TPU v7x, 512 devices: a whole 4x4x16 slice. The times are simulated.
512 devices in a mesh: grp: 4 (over y), resp: 16 (over z_lo, core), tp: 8 (over z_hi, x).
Axes of the slice: x: 4, y: 4, z: 16 (z_hi: 2, z_lo: 8; z = z_hi * 8 + z_lo), core: 2. Of those that a mesh axis runs over, the one named last changes fastest.
Arguments:
- queries: bfloat16 [8192, 64, 576], P(('grp', 'resp'), 'tp'), parts along dimension 0, may hold values from -44 to 44
- grad_out: bfloat16 [8192, 64, 512], P(('grp', 'resp'), 'tp'), parts along dimension 0, may hold values from -32 to 32
- prompt_kv: bfloat16 [3072, 576], P(('grp', 'resp')), parts along dimension 0, may hold values from -5 to 5
- resp_kv: bfloat16 [8192, 576], P(('grp', 'resp')), parts along dimension 0, may hold values from -6 to 6
- lengths: int32 [64], P(('grp', 'resp')), parts along dimension 0, may hold values from 16 to 128, as said below
Outputs:
- grad_queries: bfloat16 [8192, 64, 576], P(('grp', 'resp'), 'tp'), parts along dimension 0
- grad_prompt: bfloat16 [3072, 576], P(('grp', 'resp')), parts along dimension 0
- grad_resp: bfloat16 [8192, 576], P(('grp', 'resp')), parts along dimension 0
There are 4 independent parts, one for each index of `grp`. A program takes and returns all parts, laid end to end along the dimension named above; each array names one. Nothing has to cross between parts.
Inputs may be any that keep to these rules, and one draw needn't show every extreme that they name: `lengths`: every response has length 16 or more, and some response has length 128.
All inputs are finite; a program needn't handle non-finite values.
Results may differ from a plain program's by a relative error of at most 0.012.
Values may be sent and summed in bfloat16 or wider, within the bound.
No kernel may reach another device: no remote copies, remote signals or barrier semaphores. Data moves between devices by JAX's collectives and lax.ppermute only.
A program may use at most 64 MiB of HBM per device.

v0:
```python
import jax
import jax.numpy as jnp
from jax import lax
from jax.sharding import PartitionSpec as P

softmax_scale = 192 ** (-0.5)
masked_value = -1e30


def local_grads(queries, grad_out, prompt_all, resp_kv, length):
    rows, heads, width = queries.shape
    latent = grad_out.shape[2]
    prompt_rows = prompt_all.shape[0]
    keys = jnp.concatenate([prompt_all, resp_kv], 0)
    total = keys.shape[0]
    position = jnp.arange(rows, dtype=jnp.int32)
    key_pos = jnp.arange(total, dtype=jnp.int32) - prompt_rows
    allowed = key_pos[None, :] <= position[:, None]
    live = position < length
    q_flat = queries.reshape(rows * heads, width)
    scores = (
        jnp.dot(q_flat, keys.T, preferred_element_type=jnp.float32).reshape(rows, heads, total)
        * softmax_scale
    )
    scores = jnp.where(allowed[:, None, :], scores, masked_value)
    top = jnp.max(scores, axis=-1, keepdims=True)
    expo = jnp.exp(scores - top)
    probs = (expo / jnp.sum(expo, axis=-1, keepdims=True)).reshape(rows * heads, total)
    probs_b = probs.astype(jnp.bfloat16)
    d_flat = jnp.where(live[:, None, None], grad_out, jnp.zeros_like(grad_out)).reshape(
        rows * heads, latent
    )
    values = keys[:, :latent]
    out_vals = jnp.dot(probs_b, values, preferred_element_type=jnp.float32)
    delta = jnp.sum(d_flat.astype(jnp.float32) * out_vals, axis=-1, keepdims=True)
    d_prob = jnp.dot(d_flat, values.T, preferred_element_type=jnp.float32)
    d_score = (softmax_scale * probs * (d_prob - delta)).astype(jnp.bfloat16)
    d_query = (
        jnp.dot(d_score, keys, preferred_element_type=jnp.float32)
        .astype(jnp.bfloat16)
        .reshape(rows, heads, width)
    )
    dims = (((0,), (0,)), ((), ()))
    d_keys = lax.dot_general(d_score, q_flat, dims, preferred_element_type=jnp.float32)
    d_vals = lax.dot_general(probs_b, d_flat, dims, preferred_element_type=jnp.float32)
    d_kv = jnp.concatenate([d_keys[:, :latent] + d_vals, d_keys[:, latent:]], 1)
    return (d_query, d_kv[:prompt_rows], d_kv[prompt_rows:])


def body(queries, grad_out, prompt_kv, resp_kv, lengths):
    prompt_all = lax.all_gather(prompt_kv, "resp", axis=0, tiled=True)
    d_query, prompt_term, resp_term = local_grads(
        queries, grad_out, prompt_all, resp_kv, lengths[0]
    )
    mine = lax.psum_scatter(prompt_term, "resp", scatter_dimension=0, tiled=True)
    prompt_sum, resp_sum = lax.psum((mine, resp_term), "tp")
    grad_prompt = prompt_sum.astype(jnp.bfloat16)
    return (d_query, grad_prompt, resp_sum.astype(jnp.bfloat16))


def solution(mesh):
    return jax.shard_map(
        body,
        mesh=mesh,
        in_specs=(
            P(("grp", "resp"), "tp", None),
            P(("grp", "resp"), "tp", None),
            P(("grp", "resp"), None),
            P(("grp", "resp"), None),
            P(("grp", "resp")),
        ),
        out_specs=(
            P(("grp", "resp"), "tp", None),
            P(("grp", "resp"), None),
            P(("grp", "resp"), None),
        ),
        check_vma=False,
    )
```

profile of v0, /device:TPU:480, one launch (start us, length us, event | category | flops | bytes accessed | tf_op | source)
XLA Modules:
  0.0 270.5 jit_solution(6868184996795718049)
XLA Ops:
  7.2 0.0 copy-start.4
  7.2 0.0 reduce-scatter.4.cloned.1.call-start
  7.9 0.1 iota_compare_fusion
  8.0 0.0 copy-start
  8.0 1.1 copy.21
  9.1 0.4 broadcast_bitcast_fusion
  9.6 2.0 copy.23
  11.5 0.0 copy-done.4
  11.5 29.9 %all_gather.3 = bf16[768,576]{1,0:T(8,128)(2,1)} all-gather(bf16[48,576]{1,0:T(8,128)(2,1)S(1)} %copy-done.4), channel_id=1, replica_groups=mesh['grp'=4,'resp'=16,'tp'=8] {'resp'}, dimensions={0}, use_global_device_ids=true | all-gather | bytes 940032 | tf_op jit(solution)/shard_map/all_gather | solution.py:51
  41.4 0.0 copy-done
  41.4 0.2 select_bitcast_fusion
  41.6 1.3 copy.24
  43.0 2.2 copy.22
  45.2 3.2 %fusion.13 = (f32[1024]{0:T(1024)S(1)}, f32[1024,896]{0,1:T(8,128)S(1)}) fusion(pred[1024,896]{0,1:T(32,128)(4,1)} %copy.23, bf16[128,8,576]{2,1,0:T(8,128)(2,1)S(1)} %copy.22, bf16[128,576]{1,0:T(8,128)(2,1)S(1)} %copy.21, bf16[768,576]{1,0:T(8,128)(2,1)} %all_gather.3), kind=kOutput, calls=%fused_computation.27 | convolution fusion | flops 1061780480 | bytes 6803456 | tf_op jit(solution)/shard_map/dot_general | solution.py:22
  48.4 0.0 copy-start.1
  48.4 0.5 fusion.1
  49.0 0.7 copy-done.1
  49.6 0.3 copy-done.2
  49.9 1.4 multiply_reduce_fusion
  51.3 1.4 multiply_convert_fusion
  52.7 1.5 fusion.3
  54.2 1.4 slice_add_fusion
  55.6 1.4 fusion.2
  57.0 2.9 %copy.30 = f32[768,576]{1,0:T(8,128)} copy(f32[768,576]{0,1:T(8,128)} %fusion.2) | data formatting | bytes 3538944
  59.9 0.0 reduce-scatter.4.cloned.1.call-update
  59.9 3.9 %convolution_convert_fusion = bf16[1024,576]{0,1:T(8,128)(2,1)} fusion(bf16[1024,896]{0,1:T(8,128)(2,1)} %copy-done.5, bf16[128,576]{1,0:T(8,128)(2,1)S(1)} %copy.21, bf16[768,576]{1,0:T(8,128)(2,1)S(1)} %copy-done.3), kind=kOutput, calls=%fused_computation.11 | convolution fusion | flops 1059618816 | bytes 4046848 | tf_op jit(solution)/shard_map/dot_general | solution.py:39
  63.9 1.7 copy.26
  65.6 1.8 copy.27
  67.4 96.0 %reduce-scatter.4.cloned.1.call-done = f32[48,576]{1,0:T(8,128)} async-done(((f32[768,576]{1,0:T(8,128)}), f32[48,576]{1,0:T(8,128)}) %reduce-scatter.4.cloned.1.call-update) | async-done | bytes 110608
  163.4 1.0 copy.31
  164.5 98.4 %all-reduce.2 = (bf16[48,576]{0,1:T(8,128)(2,1)S(1)}, bf16[128,576]{0,1:T(8,128)(2,1)}) all-reduce(f32[48,576]{0,1:T(8,128)S(1)} %copy.31, f32[128,576]{0,1:T(8,128)S(1)} %pad_maximum_fusion.6), channel_id=1, replica_groups=mesh['grp'=4,'resp'=16,'tp'=8] {'tp'}, use_global_device_ids=true, to_apply=%region_4.5 | all-reduce | flops 101376 | bytes 608256 | tf_op jit(solution)/shard_map/psum | solution.py:56
  262.9 0.7 copy.28
  (9 shorter events, 0.1 us)
Async XLA Ops:
  7.2 4.4 %copy-start.4 = (bf16[48,576]{1,0:T(8,128)(2,1)S(1)}, bf16[48,576]{1,0:T(8,128)(2,1)}, u32[]{:S(2)}) copy-start(bf16[48,576]{1,0:T(8,128)(2,1)} %param.7) | copy-start | bytes 165892
  7.2 156.2 %reduce-scatter.4.cloned.1.call-start = ((), (), s32[]{:S(2)}) async-start(), calls=%async_computation.1 | async-start | bytes 2088960
  8.0 33.5 %copy-start = (bf16[128,8,512]{2,1,0:T(8,128)(2,1)S(1)}, bf16[128,8,512]{2,1,0:T(8,128)(2,1)}, u32[]{:S(2)}) copy-start(bf16[128,8,512]{2,1,0:T(8,128)(2,1)} %param.6) | copy-start | bytes 3145732
  48.4 1.2 copy-start.1
  48.4 1.5 copy-start.2
  52.7 1.5 copy-start.5
  57.0 2.9 %copy-start.3 = (bf16[768,576]{1,0:T(8,128)(2,1)S(1)}, bf16[768,576]{1,0:T(8,128)(2,1)}, u32[]{:S(2)}) copy-start(bf16[768,576]{1,0:T(8,128)(2,1)} %all_gather.3) | copy-start | bytes 2654212
Sparse Core Ops, SparseCore 0:
  60.0 103.3 reduce-scatter.3
where the time goes:
time: 271 us; the launch traced here: 270 us
  blocking collectives  128 us (47%)
  waiting for transfers between devices  96.1 us (35%)
  local copies, waits for them, and re-layouts  16.2 us (6%)
  between operations  14.8 us (5%)
  matrix products  12.8 us (5%)
    psum x1, blocking collectives, body(): prompt_sum, resp_sum = lax.psum((mine, resp_term), 'tp')  98.4 us
    unnamed x2, waiting for transfers between devices  96.1 us
    all_gather x1, blocking collectives, body(): prompt_all = lax.all_gather(prompt_kv, 'resp', axis=0, tiled=True)  29.9 us
    unnamed x18, local copies, waits for them, and re-layouts  10.8 us
  transfers between devices with their start and end apart: 1, of which 1 were waited for; matrix products, arithmetic and copies ran while one was open for 3% of the time, Pallas kernels for 0%

commit v1 on v0

--- a/solution.py
+++ b/solution.py
@@ -48,7 +48,9 @@
 
 
 def body(queries, grad_out, prompt_kv, resp_kv, lengths):
-    prompt_all = lax.all_gather(prompt_kv, "resp", axis=0, tiled=True)
+    prompt_all = jnp.concatenate(
+        lax.all_to_all(jnp.stack([prompt_kv] * lax.axis_size("resp")), "resp", 0, 0), axis=0
+    )
     d_query, prompt_term, resp_term = local_grads(
         queries, grad_out, prompt_all, resp_kv, lengths[0]
     )

time: 271 us -> 283 us (1.044)
  the two profiles are of different devices: /device:TPU:480 before, /device:TPU:24 now
where the time goes in v1:
time: 283 us; the launch traced here: 282 us
  waiting for transfers between devices  137 us (48%)
  blocking collectives  83.5 us (30%)
  local copies, waits for them, and re-layouts  16.9 us (6%)
  matrix products  15.3 us (5%)
  between operations  14.9 us (5%)
  starting transfers between devices  12.7 us (4%)
    unnamed x2, waiting for transfers between devices  102 us
    psum x1, blocking collectives, body(): prompt_sum, resp_sum = lax.psum((mine, resp_term), 'tp')  83.5 us
    all_to_all x1, waiting for transfers between devices, body(): lax.all_to_all(jnp.stack([prompt_kv] * lax.axis_size('resp')), 'resp', 0, 0)  34.5 us
    all_to_all x1, starting transfers between devices, body(): lax.all_to_all(jnp.stack([prompt_kv] * lax.axis_size('resp')), 'resp', 0, 0)  12.7 us
    unnamed x14, local copies, waits for them, and re-layouts  9.46 us
  transfers between devices with their start and end apart: 2, of which 2 were waited for; matrix products, arithmetic and copies ran while one was open for 5% of the time, Pallas kernels for 0%

profile of v1, /device:TPU:24, one launch (start us, length us, event | category | flops | bytes accessed | tf_op | source)
XLA Modules:
  0.0 282.3 jit_solution(653064335418278265)
XLA Ops:
  7.2 1.9 stack.2
  9.1 12.7 %all-to-all-start = ((bf16[16,48,576]{2,1,0:T(8,128)(2,1)}), bf16[16,48,576]{2,1,0:T(8,128)(2,1)}, u32[]{:S(2)}, u32[]{:S(2)}) async-start(bf16[16,48,576]{2,1,0:T(8,128)(2,1)} %stack.2), calls=%async_computation | async-start | bytes 1966080 | tf_op jit(solution)/shard_map/all_to_all | solution.py:52
  21.8 0.0 copy-start
  21.8 0.0 reduce-scatter.4.cloned.1.call-start
  22.5 0.2 copy.21
  22.7 0.1 iota_compare_fusion
  22.8 0.4 broadcast_bitcast_fusion
  23.2 2.0 copy.23
  25.2 0.2 select_bitcast_fusion
  25.4 1.5 copy.24
  26.9 2.2 copy.22
  29.1 34.5 %all-to-all-done = bf16[16,48,576]{2,1,0:T(8,128)(2,1)} async-done(((bf16[16,48,576]{2,1,0:T(8,128)(2,1)}), bf16[16,48,576]{2,1,0:T(8,128)(2,1)}, u32[]{:S(2)}, u32[]{:S(2)}) %all-to-all-start) | async-done | bytes 884768 | tf_op jit(solution)/shard_map/all_to_all | solution.py:52
  63.6 3.2 %fusion.13 = (f32[1024]{0:T(1024)S(1)}, f32[1024,896]{0,1:T(8,128)S(1)}) fusion(pred[1024,896]{0,1:T(32,128)(4,1)} %copy.23, bf16[128,8,576]{2,1,0:T(8,128)(2,1)S(1)} %copy.22, bf16[128,576]{1,0:T(8,128)(2,1)S(1)} %copy.21, bf16[768,576]{1,0:T(8,128)(2,1)} %bitcast.1), kind=kOutput, calls=%fused_computation.27 | convolution fusion | flops 1061780480 | bytes 6803456 | tf_op jit(solution)/shard_map/dot_general | solution.py:22
  66.8 0.0 copy-start.1
  66.8 0.5 fusion.1
  67.4 0.7 copy-done.1
  68.1 2.5 multiply_reduce_fusion
  70.6 2.5 multiply_convert_fusion
  73.1 0.0 copy-start.3
  73.1 1.5 fusion.3
  74.6 0.0 copy-done.3
  74.6 1.4 slice_add_fusion
  76.0 1.4 fusion.2
  77.4 2.8 %copy.30 = f32[768,576]{1,0:T(8,128)} copy(f32[768,576]{0,1:T(8,128)} %fusion.2) | data formatting | bytes 3538944
  80.2 0.0 reduce-scatter.4.cloned.1.call-update
  80.2 4.2 %convolution_convert_fusion = bf16[1024,576]{0,1:T(8,128)(2,1)} fusion(bf16[1024,896]{0,1:T(8,128)(2,1)} %copy-done.3, bf16[128,576]{1,0:T(8,128)(2,1)S(1)} %copy.21, bf16[768,576]{1,0:T(8,128)(2,1)} %bitcast.1), kind=kOutput, calls=%fused_computation.11 | convolution fusion | flops 1059618816 | bytes 4046848 | tf_op jit(solution)/shard_map/dot_general | solution.py:39
  84.4 1.7 copy.26
  86.1 1.8 copy.27
  87.9 102.2 %reduce-scatter.4.cloned.1.call-done = f32[48,576]{1,0:T(8,128)} async-done(((f32[768,576]{1,0:T(8,128)}), f32[48,576]{1,0:T(8,128)}) %reduce-scatter.4.cloned.1.call-update) | async-done | bytes 110608
  190.1 1.0 copy.31
  191.1 83.5 %all-reduce.2 = (bf16[48,576]{0,1:T(8,128)(2,1)S(1)}, bf16[128,576]{0,1:T(8,128)(2,1)}) all-reduce(f32[48,576]{0,1:T(8,128)S(1)} %copy.31, f32[128,576]{0,1:T(8,128)S(1)} %pad_maximum_fusion.6), channel_id=1, replica_groups=mesh['grp'=4,'resp'=16,'tp'=8] {'tp'}, use_global_device_ids=true, to_apply=%region_4.5 | all-reduce | flops 101376 | bytes 608256 | tf_op jit(solution)/shard_map/psum | solution.py:58
  274.7 0.7 copy.28
  (7 shorter events, 0.1 us)
Async XLA Ops:
  7.2 15.4 %copy-start.2 = (bf16[128,576]{0,1:T(8,128)(2,1)S(1)}, bf16[128,576]{0,1:T(8,128)(2,1)}, u32[]{:S(2)}) copy-start(bf16[128,576]{0,1:T(8,128)(2,1)} %param.8) | copy-start | bytes 442372
  9.1 54.5 %all-to-all-start = ((bf16[16,48,576]{2,1,0:T(8,128)(2,1)}), bf16[16,48,576]{2,1,0:T(8,128)(2,1)}, u32[]{:S(2)}, u32[]{:S(2)}) async-start(bf16[16,48,576]{2,1,0:T(8,128)(2,1)} %stack.2), calls=%async_computation | async-start | bytes 1966080 | tf_op jit(solution)/shard_map/all_to_all | solution.py:52
  21.8 3.5 %copy-start = (bf16[128,8,512]{2,1,0:T(8,128)(2,1)S(1)}, bf16[128,8,512]{2,1,0:T(8,128)(2,1)}, u32[]{:S(2)}) copy-start(bf16[128,8,512]{2,1,0:T(8,128)(2,1)} %param.6) | copy-start | bytes 3145732
  21.8 168.3 %reduce-scatter.4.cloned.1.call-start = ((), (), s32[]{:S(2)}) async-start(), calls=%async_computation.2 | async-start | bytes 2088960
  66.8 1.2 copy-start.1
  73.1 1.5 copy-start.3
Sparse Core Ops, SparseCore 0:
  80.3 109.7 reduce-scatter.3
